TPU v7x, 128 devices: a whole 4x4x4 slice. The times are simulated.
128 devices in a mesh: seq: 32 (over x, y, core), head: 4 (over z).
Axes of the slice: x: 4, y: 4, z: 4, core: 2. Of those that a mesh axis runs over, the one named last changes fastest.
Arguments:
- queries: bfloat16 [32768, 2048], P('seq', 'head'), may hold values from -6 to 6
- keys: bfloat16 [32768, 2048], P('seq', 'head'), may hold values from -6 to 6
- values: bfloat16 [32768, 2048], P('seq', 'head'), may hold values from -6 to 6
- out_weight: bfloat16 [4096, 2048], P('seq', 'head'), may hold values from -0.125 to 0.125
- out_grad: bfloat16 [32768, 4096], P('seq'), may hold values from -6 to 6
Outputs:
- mixed: bfloat16 [32768, 4096], P('seq', 'head')
- grad_queries: bfloat16 [32768, 2048], P('seq', 'head')
- grad_keys: bfloat16 [32768, 2048], P('seq', 'head')
- grad_values: bfloat16 [32768, 2048], P('seq', 'head')
- grad_weight: float32 [4096, 2048], P('seq', 'head')
All inputs are finite; a program needn't handle non-finite values.
Results may differ from a plain program's by a relative error of at most 0.022.
Values may be sent and summed in bfloat16 or wider, within the bound.
A program may use at most 128 MiB of HBM per device.

v0:
```python
import jax
import jax.numpy as jnp
from jax import lax
from jax.sharding import PartitionSpec as P

HEAD_DIM = 128
BLOCK = 512


EPSILON = 1e-06
FULL_PRECISION = lax.Precision.HIGHEST


def exclusive_forward(stacked):
    running = jnp.cumsum(stacked, axis=0)
    return jnp.concatenate([jnp.zeros_like(stacked[:1]), running[:-1]], axis=0)


def exclusive_backward(stacked):
    running = jnp.cumsum(stacked[::-1], axis=0)[::-1]
    return jnp.concatenate([running[1:], jnp.zeros_like(stacked[:1])], axis=0)


def per_device(queries, keys, values, out_weight, out_grad):
    tok_rows, head_cols = queries.shape
    head_count = head_cols // HEAD_DIM
    blk_count = tok_rows // BLOCK
    causal = jnp.tril(jnp.ones((BLOCK, BLOCK), dtype=bool))
    my_rank = lax.axis_index("seq")
    contract = (((1,), (1,)), ((), ()))
    full_weight = lax.all_gather(out_weight, "seq", axis=0, tiled=True)

    def blocked(array):
        return array.reshape(blk_count, BLOCK, head_count, HEAD_DIM)

    q_blocks = blocked(queries)
    k_blocks = blocked(keys)
    v_blocks = blocked(values)
    kv_state = jnp.einsum("nshe,nshf->nhef", k_blocks, v_blocks, preferred_element_type=jnp.float32)
    own_kv = jnp.sum(kv_state, axis=0)
    incoming = lax.all_gather(own_kv[None].astype(jnp.bfloat16), "seq", axis=0, tiled=True).astype(
        jnp.float32
    )
    peer_rank = jnp.arange(incoming.shape[0])
    lower_mask = (peer_rank < my_rank)[:, None, None, None]
    before = jnp.zeros_like(own_kv) + jnp.sum(jnp.where(lower_mask, incoming, 0.0), axis=0)
    states = before[None] + exclusive_forward(kv_state)
    scores = jnp.einsum("nthe,nshe->nhts", q_blocks, k_blocks, preferred_element_type=jnp.float32)
    masked = jnp.where(causal[None, None], scores, 0.0).astype(jnp.bfloat16)
    attended = jnp.einsum("nhts,nshe->nthe", masked, v_blocks, preferred_element_type=jnp.float32)
    attended = attended + jnp.einsum(
        "nthe,nhef->nthf", q_blocks.astype(jnp.float32), states, precision=FULL_PRECISION
    )
    inverse_rms = lax.rsqrt(jnp.mean(attended * attended, axis=-1, keepdims=True) + EPSILON)
    normed = (attended * inverse_rms).astype(jnp.bfloat16).reshape(tok_rows, head_cols)
    partial_value = lax.dot_general(
        normed, full_weight, contract, preferred_element_type=jnp.float32
    )
    mixed_out = lax.psum_scatter(
        partial_value.astype(jnp.bfloat16), "head", scatter_dimension=1, tiled=True
    )
    grad_normed = jnp.dot(out_grad, full_weight, preferred_element_type=jnp.float32)
    grad_normed = grad_normed.reshape(blk_count, BLOCK, head_count, HEAD_DIM)
    inner = jnp.mean(attended * grad_normed, axis=-1, keepdims=True)
    grad_attended = (inverse_rms * grad_normed - attended * inverse_rms**3 * inner).astype(
        jnp.bfloat16
    )
    qda_state = jnp.einsum(
        "nthe,nthf->nhef", q_blocks, grad_attended, preferred_element_type=jnp.float32
    )
    own_qda = jnp.sum(qda_state, axis=0)
    incoming = lax.all_gather(own_qda[None].astype(jnp.bfloat16), "seq", axis=0, tiled=True).astype(
        jnp.float32
    )
    peer_rank = jnp.arange(incoming.shape[0])
    upper_mask = (peer_rank > my_rank)[:, None, None, None]
    after = jnp.zeros_like(own_qda) + jnp.sum(jnp.where(upper_mask, incoming, 0.0), axis=0)
    futures = after[None] + exclusive_backward(qda_state)
    grad_float = grad_attended.astype(jnp.float32)
    dmask = jnp.where(
        causal[None, None],
        jnp.einsum("nthf,nshf->nhts", grad_attended, v_blocks, preferred_element_type=jnp.float32),
        0.0,
    ).astype(jnp.bfloat16)
    grad_q = jnp.einsum("nhts,nshe->nthe", dmask, k_blocks, preferred_element_type=jnp.float32)
    grad_q = grad_q + jnp.einsum("nthf,nhef->nthe", grad_float, states, precision=FULL_PRECISION)
    grad_k = jnp.einsum("nhts,nthe->nshe", dmask, q_blocks, preferred_element_type=jnp.float32)
    grad_k = grad_k + jnp.einsum(
        "nshf,nhef->nshe", v_blocks.astype(jnp.float32), futures, precision=FULL_PRECISION
    )
    grad_v = jnp.einsum(
        "nhts,nthf->nshf", masked, grad_attended, preferred_element_type=jnp.float32
    )
    grad_v = grad_v + jnp.einsum(
        "nshe,nhef->nshf", k_blocks.astype(jnp.float32), futures, precision=FULL_PRECISION
    )
    grad_weight = lax.psum_scatter(
        lax.dot_general(
            out_grad, normed, (((0,), (0,)), ((), ())), preferred_element_type=jnp.float32
        ).astype(jnp.bfloat16),
        "seq",
        scatter_dimension=0,
        tiled=True,
    ).astype(jnp.float32)
    return (
        mixed_out,
        grad_q.astype(jnp.bfloat16).reshape(tok_rows, head_cols),
        grad_k.astype(jnp.bfloat16).reshape(tok_rows, head_cols),
        grad_v.astype(jnp.bfloat16).reshape(tok_rows, head_cols),
        grad_weight,
    )


def solution(mesh):
    in_specs = (
        P("seq", "head"),
        P("seq", "head"),
        P("seq", "head"),
        P("seq", "head"),
        P("seq", None),
    )
    out_specs = (
        P("seq", "head"),
        P("seq", "head"),
        P("seq", "head"),
        P("seq", "head"),
        P("seq", "head"),
    )
    return jax.shard_map(
        per_device, mesh=mesh, in_specs=in_specs, out_specs=out_specs, check_vma=False
    )
```

profile of v0, /device:TPU:1, one launch (start us, length us, event | category | flops | bytes accessed | tf_op | source)
XLA Modules:
  0.0 352.2 jit_solution(14475033522570819331)
XLA Ops:
  7.9 1.3 reshape.88
  9.3 1.7 reshape.89
  11.1 2.0 fusion.31
  13.1 1.3 reshape.87
  17.1 1.4 select_convert_fusion.1
  18.5 1.9 copy-done
  20.4 2.8 fusion.11
  23.2 36.7 %all-gather.6.cloned.1.call-done = bf16[4096,512]{1,0:T(8,128)(2,1)} async-done(((bf16[128,512]{1,0:T(8,128)(2,1)}), bf16[4096,512]{1,0:T(8,128)(2,1)}) %all-gather.6.cloned.1.call-update) | async-done | bytes 4194320 | tf_op jit(solution)/shard_map/all_gather | solution.py:31
  59.9 8.1 %fusion.34 = f32[1024,512]{1,0:T(8,128)S(1)} fusion(bf16[1024,4096]{1,0:T(8,128)(2,1)} %param.9, bf16[4096,512]{1,0:T(8,128)(2,1)} %all-gather.6.cloned.1.call-done), kind=kOutput, calls=%fused_computation.60 | convolution fusion | flops 4294967296 | bytes 14680064 | tf_op jit(solution)/shard_map/dot_general | solution.py:62
  68.0 1.7 reshape.91
  69.7 1.9 copy.91
  71.7 36.4 %all-gather.8.cloned.1.call-done = bf16[128,128,128]{2,1,0:T(8,128)(2,1)} async-done(((bf16[4,128,128]{2,1,0:T(8,128)(2,1)}), bf16[128,128,128]{2,1,0:T(8,128)(2,1)}) %all-gather.8.cloned.1.call-update) | async-done | bytes 4194320 | tf_op jit(solution)/shard_map/all_gather | solution.py:41
  108.1 3.4 fusion.1
  111.5 2.4 multiply_reduce_fusion
  114.0 2.0 subtract_convert_fusion
  116.0 1.7 copy.90
  117.7 9.5 %fusion.2 = bf16[4096,512]{0,1:T(8,128)(2,1)} fusion(bf16[1024,4096]{1,0:T(8,128)(2,1)} %param.9, bf16[128,8,4,128]{3,2,1,0:T(4,128)(2,1)S(1)} %bitcast.71), kind=kOutput, calls=%fused_computation.8 | convolution fusion | flops 4297064448 | bytes 13631488 | tf_op jit(solution)/shard_map/dot_general | solution.py:98
  127.2 6.5 %copy.118 = bf16[4096,512]{1,0:T(8,128)(2,1)} copy(bf16[4096,512]{0,1:T(8,128)(2,1)} %fusion.2) | data formatting | bytes 8388608
  137.0 9.0 %convolution_convert_fusion = bf16[1024,4096]{1,0:T(8,128)(2,1)} fusion(bf16[4096,512]{1,0:T(8,128)(2,1)} %all-gather.6.cloned.1.call-done, bf16[128,8,4,128]{3,2,1,0:T(4,128)(2,1)S(1)} %bitcast.72), kind=kOutput, calls=%fused_computation.6 | convolution fusion | flops 4299161600 | bytes 13631488 | tf_op jit(solution)/shard_map/dot_general | solution.py:56
  146.0 2.0 rev.4
  148.0 2.5 select_convert_fusion
  150.5 1.2 fusion.19
  151.8 1.3 fusion.4
  155.0 2.0 fusion.35
  157.0 2.9 fusion.23
  159.9 53.1 %reduce-scatter.7.cloned.1.call-done = bf16[128,512]{1,0:T(8,128)(2,1)} async-done(((bf16[4096,512]{1,0:T(8,128)(2,1)}), bf16[128,512]{1,0:T(8,128)(2,1)}) %reduce-scatter.7.cloned.1.call-update) | async-done | bytes 131088
  214.9 47.9 %all-gather.10.cloned.1.call-done = bf16[128,128,128]{2,1,0:T(8,128)(2,1)} async-done(((bf16[4,128,128]{2,1,0:T(8,128)(2,1)}), bf16[128,128,128]{2,1,0:T(8,128)(2,1)}) %all-gather.10.cloned.1.call-update) | async-done | bytes 4194320 | tf_op jit(solution)/shard_map/all_gather | solution.py:72
  262.8 3.3 fusion
  266.4 3.6 %fusion.5 = bf16[2,512,4,128]{1,3,2,0:T(8,128)(2,1)} fusion(f32[2,4,128,512]{3,2,1,0:T(8,128)} %fusion.35, f32[2,4,128,128]{2,3,1,0:T(8,128)S(1)} %fusion.6, bf16[2,512,4,128]{3,2,1,0:T(4,128)(2,1)S(1)} %copy-done.7), kind=kOutput, calls=%fused_computation.19 | convolution fusion | flops 806354944 | bytes 4718592 | tf_op jit(solution)/shard_map/nshe,nhef->nshf/dot_general | solution.py:94
  270.0 1.9 copy.109
  273.1 3.2 fusion.3
  278.3 67.4 %reduce-scatter.5.cloned.1.call-done = bf16[1024,1024]{1,0:T(8,128)(2,1)} async-done(((bf16[1024,4096]{1,0:T(8,128)(2,1)}), bf16[1024,1024]{1,0:T(8,128)(2,1)}) %reduce-scatter.5.cloned.1.call-update) | async-done | bytes 2097168 | tf_op jit(solution)/shard_map/reduce_scatter | solution.py:59
  (52 shorter events, 13.9 us)
Async XLA Ops:
  7.2 52.7 %all-gather.6.cloned.1.call-start = ((), (), s32[]{:S(2)}) async-start(), calls=%async_computation.2 | async-start | bytes 4325376 | tf_op jit(solution)/shard_map/all_gather | solution.py:31
  7.9 100.2 %all-gather.8.cloned.1.call-start = ((), (), s32[]{:S(2)}) async-start(), calls=%async_computation.4 | async-start | bytes 4325376 | tf_op jit(solution)/shard_map/all_gather | solution.py:41
  9.3 7.1 %copy-start.5 = (bf16[2,512,4,128]{3,2,1,0:T(4,128)(2,1)}, bf16[2,512,4,128]{3,2,1,0:T(4,128)(2,1)S(1)}, u32[]{:S(2)}) copy-start(bf16[2,512,4,128]{3,2,1,0:T(4,128)(2,1)S(1)} %reshape.88) | copy-start | bytes 3145732
  11.0 7.4 %copy-start.3 = (bf16[2,512,4,128]{3,2,1,0:T(4,128)(2,1)}, bf16[2,512,4,128]{3,2,1,0:T(4,128)(2,1)S(1)}, u32[]{:S(2)}) copy-start(bf16[2,512,4,128]{3,2,1,0:T(4,128)(2,1)S(1)} %reshape.89) | copy-start | bytes 3145732
  13.1 200.0 %reduce-scatter.7.cloned.1.call-start = ((), (), s32[]{:S(2)}) async-start(), calls=%async_computation.6 | async-start | bytes 4325376
  16.4 0.7 copy-start.11
  18.5 1.9 copy-start
  108.1 3.4 copy-start.8
  133.7 1.2 copy-start.2
  133.7 129.1 %all-gather.10.cloned.1.call-start = ((), (), s32[]{:S(2)}) async-start(), calls=%async_computation.5 | async-start | bytes 4325376 | tf_op jit(solution)/shard_map/all_gather | solution.py:72
  136.9 208.8 %reduce-scatter.5.cloned.1.call-start = ((), (), s32[]{:S(2)}) async-start(), calls=%async_computation.3 | async-start | bytes 10485760 | tf_op jit(solution)/shard_map/reduce_scatter | solution.py:59
  146.0 2.0 copy-start.4
  148.0 2.5 copy-start.6
  150.5 1.3 copy-start.9
  151.8 3.2 copy-start.1
  159.9 106.3 %copy-start.10 = (f32[2,4,128,128]{2,3,1,0:T(8,128)S(1)}, f32[2,4,128,128]{2,3,1,0:T(8,128)}, u32[]{:S(2)}) copy-start(f32[2,4,128,128]{2,3,1,0:T(8,128)} %rev.4) | copy-start | bytes 1572868
  159.9 106.3 %copy-start.12 = (pred[2]{0:T(512)(128)(4,1)S(1)}, pred[2]{0:T(512)(128)(4,1)}, u32[]{:S(2)}) copy-start(pred[2]{0:T(512)(128)(4,1)} %constant.23.clone.1) | copy-start | bytes 10
  159.9 106.5 %copy-start.7 = (bf16[2,512,4,128]{3,2,1,0:T(4,128)(2,1)S(1)}, bf16[2,512,4,128]{3,2,1,0:T(4,128)(2,1)}, u32[]{:S(2)}) copy-start(bf16[2,512,4,128]{3,2,1,0:T(4,128)(2,1)} %copy-done.5) | copy-start | bytes 3145732
Sparse Core Ops, SparseCore 0:
  10.3 49.5 all-gather.5
  62.7 45.3 all-gather.7
  133.8 79.1 reduce-scatter.6
  215.4 47.3 all-gather.9
  265.9 79.7 reduce-scatter.4
where the time goes:
time: 353 us; the launch traced here: 352 us
  waiting for transfers between devices  242 us (69%)
  matrix products  53.2 us (15%)
  local copies, waits for them, and re-layouts  32.3 us (9%)
  between operations  14.1 us (4%)
  other arithmetic  10 us (3%)
    reduce_scatter x1, waiting for transfers between devices, per_device(): lax.psum_scatter(partial_value.astype(jnp.bfloat16), 'head', scatter_dime...  67.4 us
    unnamed x6, waiting for transfers between devices  53.9 us
    all_gather x1, waiting for transfers between devices, per_device(): lax.all_gather(own_qda[None].astype(jnp.bfloat16), 'seq', axis=0, tiled=T...  47.9 us
    all_gather x1, waiting for transfers between devices, per_device(): full_weight = lax.all_gather(out_weight, 'seq', axis=0, tiled=True)  36.7 us
    all_gather x1, waiting for transfers between devices, per_device(): lax.all_gather(own_kv[None].astype(jnp.bfloat16), 'seq', axis=0, tiled=True)  36.4 us
    unnamed x32, local copies, waits for them, and re-layouts  15.4 us
    dot_general x1, matrix products, per_device(): lax.dot_general(out_grad, normed, (((0,), (0,)), ((), ())), preferred_ele...  9.5 us
    dot_general x1, matrix products, per_device(): lax.dot_general(normed, full_weight, contract, preferred_element_type=jnp...  8.98 us
  transfers between devices with their start and end apart: 5, of which 5 were waited for; matrix products, arithmetic and copies ran while one was open for 19% of the time, Pallas kernels for 0%

commit v1 on v0

v1 whole, which is shorter than its diff:
```python
import jax
import jax.numpy as jnp
from jax import lax
from jax.experimental import pallas as pl
from jax.experimental.pallas import tpu as pltpu
from jax.sharding import PartitionSpec as P

HEAD_DIM = 128
HEADS = 4
CHUNK = 256
CHUNKS = 4
TOK = 1024
COLS = 512
WIDTH = 4096
EPSILON = 1e-06
MESH = pl.DeviceIdType.MESH
F32 = jnp.float32
BF16 = jnp.bfloat16


def nn(a, b):
    return lax.dot_general(a, b, (((1,), (0,)), ((), ())), preferred_element_type=F32)


def nt(a, b):
    return lax.dot_general(a, b, (((1,), (1,)), ((), ())), preferred_element_type=F32)


def tn(a, b):
    return lax.dot_general(a, b, (((0,), (0,)), ((), ())), preferred_element_type=F32)


def kernel(
    q_hbm, k_hbm, v_hbm, w_hbm, og_hbm,
    mixed_hbm, gq_hbm, gk_hbm, gv_hbm, gw_hbm,
    q, k, v, og, wc, quarter, wr, nb, normed_t, att, nf, inv,
    kvs, states, ga, qdas, futures, own_state, slices, total, totals, offset, before,
    pt, r0, ra, rb, qa, qb, r2a, r2b, mixed, gq, gk, gv, gw,
    load_sem, out_sem,
    wc1_s, wc1_r, wc2_s, wc2_r, wcs_s, wcs_r,
    wq_s, wq_r, wz_s, wz_r, wr1_s, wr1_r, wr2_s, wr2_r, wrs_s, wrs_r,
    sc1_s, sc1_r, sc2_s, sc2_r, sc3_s, sc3_r,
    zs_s, zs_r, zf_s, zf_r,
    rs0_s, rs0_r, rs1_s, rs1_r, rs2_s, rs2_r,
):
    seq = lax.axis_index("seq")
    z = lax.axis_index("head")
    x, y, c = seq // 8, (seq // 2) % 4, seq % 2
    eighth = y * 2 + c

    def at(x_, y_, c_, z_):
        return (x_ * 8 + y_ * 2 + c_, z_)

    def x_dev(d):
        return at((x + d) % 4, y, c, z)

    def y_dev(d):
        return at(x, (y + d) % 4, c, z)

    def z_dev(d):
        return (seq, (z + d) % 4)

    def group_dev(m):
        other = (eighth + m) % 8
        return at(x, other // 2, other % 2, z)

    sibling = at(x, y, 1 - c, z)

    def remote(src, dst, send, recv, device):
        return pltpu.make_async_remote_copy(
            src_ref=src, dst_ref=dst, send_sem=send, recv_sem=recv,
            device_id=device, device_id_type=MESH,
        )

    pending = []

    def go(copies):
        for copy in copies:
            copy.start()
            pending.append(copy)
        return copies

    def arrived(copies):
        for copy in copies:
            copy.wait_recv()

    loads = [
        pltpu.make_async_copy(w_hbm, wc.at[x, y, c], load_sem.at[0]),
        pltpu.make_async_copy(k_hbm, k, load_sem.at[1]),
        pltpu.make_async_copy(v_hbm, v, load_sem.at[2]),
        pltpu.make_async_copy(q_hbm, q, load_sem.at[3]),
        pltpu.make_async_copy(og_hbm, og, load_sem.at[4]),
    ]
    for load in loads:
        load.start()

    barrier = pltpu.get_barrier_semaphore()
    partners = [x_dev(1), x_dev(2), x_dev(3), z_dev(1), z_dev(2), z_dev(3)]
    partners += [group_dev(m) for m in range(1, 8)]
    for partner in partners:
        pl.semaphore_signal(barrier, inc=1, device_id=partner, device_id_type=MESH)
    pl.semaphore_wait(barrier, len(partners))

    loads[0].wait()
    wc_first = go(
        [
            remote(
                wc.at[x, y, c, pl.ds(0, 64)], wc.at[x, y, c, pl.ds(0, 64)],
                wc1_s.at[d - 1], wc1_r.at[d - 1], x_dev(d),
            )
            for d in (1, 3, 2)
        ]
        + [
            remote(
                wc.at[x, y, c, pl.ds(64, 64)], wc.at[x, y, c, pl.ds(64, 64)],
                wc1_s.at[2 + d], wc1_r.at[2 + d], y_dev(d),
            )
            for d in (1, 3, 2)
        ]
    )

    def quarter_rows(part):
        return pl.ds(pl.multiple_of(part * 32, 32), 32)

    quarters = go(
        [
            remote(
                wc.at[x, y, c, quarter_rows((x + d) % 4)], quarter.at[x],
                wq_s.at[d - 1], wq_r.at[d - 1], x_dev(d),
            )
            for d in (1, 3, 2)
        ]
    )
    quarter[x] = wc[x, y, c, quarter_rows(x), :]

    def rows_of(t):
        return pl.ds(pl.multiple_of(t * CHUNK, CHUNK), CHUNK)

    def head_cols(h):
        return slice(h * HEAD_DIM, (h + 1) * HEAD_DIM)

    loads[1].wait()
    loads[2].wait()

    @pl.loop(0, CHUNKS)
    def _(t):
        for h in range(HEADS):
            kvs[t, h] = tn(k[rows_of(t), head_cols(h)], v[rows_of(t), head_cols(h)])

    def publish(n, source):
        for h in range(HEADS):
            state = source[0, h] + source[1, h] + source[2, h] + source[3, h]
            own_state[n, 2 * h] = state[:64].astype(BF16)
            own_state[n, 2 * h + 1] = state[64:].astype(BF16)

    def scan_first(n):
        copies = go(
            [
                remote(
                    own_state.at[n, (eighth + m) % 8], slices.at[n, eighth],
                    sc1_s.at[n, m - 1], sc1_r.at[n, m - 1], group_dev(m),
                )
                for m in range(1, 8)
            ]
        )
        slices[n, eighth] = own_state[n, eighth]
        return copies

    def scan_second(n):
        running = slices[n, 0].astype(F32)
        for i in range(1, 8):
            running = running + slices[n, i].astype(F32)
        total[n] = running.astype(BF16)
        totals[n, x] = total[n]
        return go(
            [
                remote(
                    total.at[n], totals.at[n, x],
                    sc2_s.at[n, d - 1], sc2_r.at[n, d - 1], x_dev(d),
                )
                for d in (1, 3, 2)
            ]
        )

    def scan_third(n):
        base = jnp.zeros((64, HEAD_DIM), F32)
        for i in range(4):
            counts = (x > i) if n == 0 else (x < i)
            base = base + jnp.where(counts, totals[n, i].astype(F32), 0.0)
        order = range(8) if n == 0 else range(7, -1, -1)
        for i in order:
            offset[n, i] = base.astype(BF16)
            base = base + slices[n, i].astype(F32)
        copies = go(
            [
                remote(
                    offset.at[n, (eighth + m) % 8], before.at[n, eighth],
                    sc3_s.at[n, m - 1], sc3_r.at[n, m - 1], group_dev(m),
                )
                for m in range(1, 8)
            ]
        )
        before[n, eighth] = offset[n, eighth]
        return copies

    def incoming(n, h):
        return jnp.concatenate(
            [before[n, 2 * h].astype(F32), before[n, 2 * h + 1].astype(F32)], axis=0
        )

    publish(0, kvs)
    step = scan_first(0)

    row = lax.broadcasted_iota(jnp.int32, (CHUNK, CHUNK), 0)
    col = lax.broadcasted_iota(jnp.int32, (CHUNK, CHUNK), 1)

    def lower(scores):
        return jnp.where(row >= col, scores, 0.0).astype(BF16)

    def upper(scores):
        return jnp.where(row <= col, scores, 0.0).astype(BF16)

    def intra(t):
        for h in range(HEADS):
            qh, kh = q[rows_of(t), head_cols(h)], k[rows_of(t), head_cols(h)]
            att[rows_of(t), head_cols(h)] = nn(lower(nt(qh, kh)), v[rows_of(t), head_cols(h)])

    loads[3].wait()
    pl.loop(0, 2)(intra)
    arrived(step)
    step = scan_second(0)

    arrived(wc_first)
    wc_second = go(
        [
            remote(
                wc.at[:, y, c, pl.ds(0, 64)], wc.at[:, y, c, pl.ds(0, 64)],
                wc2_s.at[d - 1], wc2_r.at[d - 1], y_dev(d),
            )
            for d in (1, 3, 2)
        ]
        + [
            remote(
                wc.at[x, :, c, pl.ds(64, 64)], wc.at[x, :, c, pl.ds(64, 64)],
                wc2_s.at[2 + d], wc2_r.at[2 + d], x_dev(d),
            )
            for d in (1, 3, 2)
        ]
    )
    arrived(quarters)
    to_layer = go(
        [
            remote(
                quarter.at[(z + d) % 4], wr.at[3 - d, y, c, x],
                wz_s.at[d - 1], wz_r.at[d - 1], z_dev(d),
            )
            for d in (1, 3, 2)
        ]
    )

    pl.loop(2, 4)(intra)
    arrived(step)
    step = scan_third(0)
    arrived(to_layer)
    wr_first = go(
        [
            remote(
                wr.at[:, y, c, x, pl.ds(0, 16)], wr.at[:, y, c, x, pl.ds(0, 16)],
                wr1_s.at[d - 1], wr1_r.at[d - 1], x_dev(d),
            )
            for d in (1, 3, 2)
        ]
        + [
            remote(
                wr.at[:, y, c, x, pl.ds(16, 16)], wr.at[:, y, c, x, pl.ds(16, 16)],
                wr1_s.at[2 + d], wr1_r.at[2 + d], y_dev(d),
            )
            for d in (1, 3, 2)
        ]
    )
    arrived(step)

    for h in range(HEADS):
        state = incoming(0, h)
        for t in range(CHUNKS):
            states[t, h] = state.astype(BF16)
            state = state + kvs[t, h]

    def z_send(t, way):
        return remote(
            nb.at[0, rows_of(t)], nb.at[3 if way == 0 else 1, rows_of(t)],
            zs_s.at[way, t], zs_r.at[way, t], z_dev(1 if way == 0 else 3),
        )

    def z_forward(t, way):
        part = pl.ds(pl.multiple_of(t * CHUNK + way * 128, 128), 128)
        return remote(
            nb.at[3 if way == 0 else 1, part], nb.at[2, part],
            zf_s.at[way, t], zf_r.at[way, t], z_dev(1 if way == 0 else 3),
        )

    def forward(t):
        for way in (0, 1):
            z_send(t, way).wait_recv()
            z_forward(t, way).start()

    @pl.loop(0, CHUNKS)
    def _(t):
        for h in range(HEADS):
            a = att[rows_of(t), head_cols(h)] + nn(q[rows_of(t), head_cols(h)], states[t, h])
            scale = lax.rsqrt(jnp.mean(a * a, axis=-1, keepdims=True) + EPSILON)
            n = a * scale
            nf[rows_of(t), head_cols(h)] = n
            inv[rows_of(t), head_cols(h)] = jnp.broadcast_to(scale, n.shape)
            nb[0, rows_of(t), head_cols(h)] = n.astype(BF16)
            normed_t[t, head_cols(h), :] = n.T.astype(BF16)
        for way in (0, 1):
            z_send(t, way).start()

    arrived(wr_first)
    wr_second = go(
        [
            remote(
                wr.at[:, y, c, :, pl.ds(0, 16)], wr.at[:, y, c, :, pl.ds(0, 16)],
                wr2_s.at[d - 1], wr2_r.at[d - 1], y_dev(d),
            )
            for d in (1, 3, 2)
        ]
        + [
            remote(
                wr.at[:, :, c, x, pl.ds(16, 16)], wr.at[:, :, c, x, pl.ds(16, 16)],
                wr2_s.at[2 + d], wr2_r.at[2 + d], x_dev(d),
            )
            for d in (1, 3, 2)
        ]
    )

    def pair_copy(i):
        return remote(
            pt.at[i, 1 - c], r0.at[i], rs0_s.at[i], rs0_r.at[i], sibling
        )

    loads[4].wait()

    @pl.loop(0, 16)
    def _(n):
        i = (x * 4 + 4 + n) % 16
        block = og[:, pl.ds(pl.multiple_of(i * 256, 256), 256)]
        result = nn(normed_t[0], block[:CHUNK])
        for t in range(1, CHUNKS):
            result = result + nn(normed_t[t], block[t * CHUNK:(t + 1) * CHUNK])
        result = result.astype(BF16)
        pt[i, 0] = result[:, :128]
        pt[i, 1] = result[:, 128:]
        pair_copy(i).start()

    arrived(wc_second)
    wc_last = go([remote(wc.at[:, :, c], wc.at[:, :, c], wcs_s.at[0], wcs_r.at[0], sibling)])

    def x_part(d):
        return remote(
            pt.at[pl.ds(pl.multiple_of((x + d) % 4 * 4, 4), 4), c, pl.ds(0, 256)], ra.at[d - 1],
            rs1_s.at[0, d - 1], rs1_r.at[0, d - 1], x_dev(d),
        )

    for d in range(1, 5):
        @pl.loop(0, 4)
        def _(j):
            i = (x + d) % 4 * 4 + j
            pair_copy(i).wait_recv()
            pt[i, c] = (pt[i, c].astype(F32) + r0[i].astype(F32)).astype(BF16)

        if d < 4:
            x_part(d).start()

    def y_part(d, x_):
        return remote(
            pt.at[x_ * 4 + (y + d) % 4, c, pl.ds(256, 256)], rb.at[d - 1, x_],
            rs1_s.at[d, x_], rs1_r.at[d, x_], y_dev(d),
        )

    for d in (1, 3, 2):
        for x_ in range(4):
            y_part(d, x_).start()

    forward(0)

    arrived(wc_last)

    @pl.loop(0, CHUNKS)
    def _(t):
        g_all = nn(og[rows_of(t), :], wc[...].reshape(WIDTH, COLS))
        for h in range(HEADS):
            g = g_all[:, head_cols(h)]
            n = nf[rows_of(t), head_cols(h)]
            inner = jnp.mean(n * g, axis=-1, keepdims=True)
            grad = (inv[rows_of(t), head_cols(h)] * (g - n * inner)).astype(BF16)
            ga[rows_of(t), head_cols(h)] = grad
            qdas[t, h] = tn(q[rows_of(t), head_cols(h)], grad)

    publish(1, qdas)
    step = scan_first(1)
    forward(1)

    for d in range(1, 4):
        x_part(d).wait_recv()
    for j in range(4):
        summed = pt[x * 4 + j, c, :256, :].astype(F32)
        for d in range(3):
            summed = summed + ra[d, j].astype(F32)
        qa[j] = summed.astype(BF16)

    def x_final(d):
        return remote(
            qb.at[(x + d) % 4], r2b.at[d - 1], rs2_s.at[1, d - 1], rs2_r.at[1, d - 1], x_dev(d)
        )

    def y_final(d):
        return remote(
            qa.at[(y + d) % 4], r2a.at[d - 1], rs2_s.at[0, d - 1], rs2_r.at[0, d - 1], y_dev(d)
        )

    finals = go([y_final(d) for d in (1, 3, 2)])
    arrived(step)
    step = scan_second(1)
    for d in range(1, 4):
        for x_ in range(4):
            y_part(d, x_).wait_recv()
    for j in range(4):
        summed = pt[j * 4 + y, c, 256:, :].astype(F32)
        for d in range(3):
            summed = summed + rb[d, j].astype(F32)
        qb[j] = summed.astype(BF16)
    finals += go([x_final(d) for d in (1, 3, 2)])
    arrived(step)
    step = scan_third(1)

    arrived(wr_second)
    wr_last = go([remote(wr.at[:, :, c], wr.at[:, :, c], wrs_s.at[0], wrs_r.at[0], sibling)])
    forward(2)
    arrived(step)

    for h in range(HEADS):
        state = incoming(1, h)
        for t in range(CHUNKS - 1, -1, -1):
            futures[t, h] = state.astype(BF16)
            state = state + qdas[t, h]

    @pl.loop(0, CHUNKS)
    def _(t):
        for h in range(HEADS):
            where = (rows_of(t), head_cols(h))
            qh, kh, vh, gh = q[where], k[where], v[where], ga[where]
            dmask = lower(nt(gh, vh))
            gq[where] = (nn(dmask, kh) + nt(gh, states[t, h])).astype(BF16)
            dmask_t = upper(nt(vh, gh))
            gk[where] = (nn(dmask_t, qh) + nt(vh, futures[t, h])).astype(BF16)
            masked_t = upper(nt(kh, qh))
            gv[where] = (nn(masked_t, gh) + nn(kh, futures[t, h])).astype(BF16)

    stores = [
        pltpu.make_async_copy(gq, gq_hbm, out_sem.at[0]),
        pltpu.make_async_copy(gk, gk_hbm, out_sem.at[1]),
        pltpu.make_async_copy(gv, gv_hbm, out_sem.at[2]),
    ]
    for store in stores:
        store.start()

    forward(3)

    arrived(finals)
    for half, own, others in ((0, qa[y], r2a), (1, qb[x], r2b)):
        summed = own.astype(F32)
        for d in range(3):
            summed = summed + others[d].astype(F32)
        gw[:, half * 256:(half + 1) * 256] = summed.T
    stores.append(pltpu.make_async_copy(gw, gw_hbm, out_sem.at[3]))
    stores[-1].start()

    arrived(wr_last)

    def out_copy(t):
        return pltpu.make_async_copy(
            mixed.at[rows_of(t)], mixed_hbm.at[rows_of(t)], out_sem.at[4 + t]
        )

    @pl.loop(0, CHUNKS)
    def _(t):
        result = nt(nb[0, rows_of(t)], wc[z].reshape(TOK, COLS))
        for d in (1, 3):
            result = result + nt(nb[d, rows_of(t)], wr[d - 1].reshape(TOK, COLS))
        for way in (0, 1):
            z_forward(t, way).wait_recv()
        result = result + nt(nb[2, rows_of(t)], wr[1].reshape(TOK, COLS))
        mixed[rows_of(t), :] = result.astype(BF16)
        out_copy(t).start()

    for copy in pending:
        copy.wait_send()

    @pl.loop(0, CHUNKS)
    def _(t):
        for way in (0, 1):
            z_send(t, way).wait_send()
            z_forward(t, way).wait_send()
        out_copy(t).wait()

    @pl.loop(0, 16)
    def _(i):
        pair_copy(i).wait_send()

    for d in range(1, 4):
        x_part(d).wait_send()
        for x_ in range(4):
            y_part(d, x_).wait_send()
    for store in stores:
        store.wait()


def per_device(queries, keys, values, out_weight, out_grad):
    dma = pltpu.SemaphoreType.DMA
    vm = pltpu.VMEM
    scratch = [
        vm((TOK, COLS), BF16),
        vm((TOK, COLS), BF16),
        vm((TOK, COLS), BF16),
        vm((TOK, WIDTH), BF16),
        vm((4, 4, 2, 128, COLS), BF16),
        vm((4, 32, COLS), BF16),
        vm((3, 4, 2, 4, 32, COLS), BF16),
        vm((4, TOK, COLS), BF16),
        vm((CHUNKS, COLS, CHUNK), BF16),
        vm((TOK, COLS), F32),
        vm((TOK, COLS), F32),
        vm((TOK, COLS), F32),
        vm((CHUNKS, HEADS, 128, 128), F32),
        vm((CHUNKS, HEADS, 128, 128), BF16),
        vm((TOK, COLS), BF16),
        vm((CHUNKS, HEADS, 128, 128), F32),
        vm((CHUNKS, HEADS, 128, 128), BF16),
        vm((2, 8, 64, 128), BF16),
        vm((2, 8, 64, 128), BF16),
        vm((2, 64, 128), BF16),
        vm((2, 4, 64, 128), BF16),
        vm((2, 8, 64, 128), BF16),
        vm((2, 8, 64, 128), BF16),
        vm((16, 2, COLS, 128), BF16),
        vm((16, COLS, 128), BF16),
        vm((3, 4, 256, 128), BF16),
        vm((3, 4, 256, 128), BF16),
        vm((4, 256, 128), BF16),
        vm((4, 256, 128), BF16),
        vm((3, 256, 128), BF16),
        vm((3, 256, 128), BF16),
        vm((TOK, 1024), BF16),
        vm((TOK, COLS), BF16),
        vm((TOK, COLS), BF16),
        vm((TOK, COLS), BF16),
        vm((128, COLS), F32),
        dma((5,)),
        dma((8,)),
    ]
    pairs = [
        (6,), (6,), (1,),
        (3,), (3,), (6,), (6,), (1,),
        (2, 7), (2, 3), (2, 7),
        (2, CHUNKS), (2, CHUNKS),
        (16,), (4, 4), (2, 3),
    ]
    for shape in pairs:
        scratch += [dma(shape), dma(shape)]
    anywhere = pl.BlockSpec(memory_space=pl.ANY)
    return pl.pallas_call(
        kernel,
        out_shape=(
            jax.ShapeDtypeStruct((TOK, 1024), BF16),
            jax.ShapeDtypeStruct((TOK, COLS), BF16),
            jax.ShapeDtypeStruct((TOK, COLS), BF16),
            jax.ShapeDtypeStruct((TOK, COLS), BF16),
            jax.ShapeDtypeStruct((128, COLS), F32),
        ),
        in_specs=[anywhere] * 5,
        out_specs=(anywhere,) * 5,
        scratch_shapes=scratch,
        compiler_params=pltpu.CompilerParams(
            collective_id=0, has_side_effects=True, vmem_limit_bytes=60 << 20
        ),
    )(queries, keys, values, out_weight, out_grad)


def solution(mesh):
    in_specs = (
        P("seq", "head"),
        P("seq", "head"),
        P("seq", "head"),
        P("seq", "head"),
        P("seq", None),
    )
    out_specs = (
        P("seq", "head"),
        P("seq", "head"),
        P("seq", "head"),
        P("seq", "head"),
        P("seq", "head"),
    )
    return jax.shard_map(
        per_device, mesh=mesh, in_specs=in_specs, out_specs=out_specs, check_vma=False
    )
```

time: 353 us -> 87.7 us (0.25)
  waiting for transfers between devices: 242 us -> 0 us
  Pallas kernels: 0 us -> 79.5 us
  matrix products: 53.2 us -> 0 us
  local copies, waits for them, and re-layouts: 32.3 us -> 7.42 us
  between operations: 14.1 us -> 0.65 us
  other arithmetic: 10 us -> 0 us
    all_gather x3 -> x0, waiting for transfers between devices: 121 us -> none  [the longest x1 47.9 us: per_device(): lax.all_gather(own_qda[None].astype(jnp.bfloat16), 'seq', axis=0, tiled=T...]
    pallas_call x0 -> x1, Pallas kernels: none -> 79.5 us  [per_device(): pl.pallas_call(kernel, out_shape=(jax.ShapeDtypeStruct((TOK, 1024), BF16)...]
    reduce_scatter x1 -> x0, waiting for transfers between devices: 67.4 us -> none  [per_device(): lax.psum_scatter(partial_value.astype(jnp.bfloat16), 'head', scatter_dime...]
    unnamed x6 -> x0, waiting for transfers between devices: 53.9 us -> none
    dot_general x15 -> x0, matrix products: 53.2 us -> none  [the longest x1 9.5 us: per_device(): lax.dot_general(out_grad, normed, (((0,), (0,)), ((), ())), preferred_ele...]
    reshape x5 -> x0, local copies, waits for them, and re-layouts: 8.06 us -> none  [the longest x3 4.41 us: blocked(): return array.reshape(blk_count, BLOCK, head_count, HEAD_DIM)]
    unnamed x32 -> x13, local copies, waits for them, and re-layouts: 15.4 us -> 7.42 us
    reduce_sum x2 -> x0, other arithmetic: 6.7 us -> none  [the longest x1 3.42 us: per_device(): jnp.sum(jnp.where(lower_mask, incoming, 0.0), axis=0)]
  transfers between devices with their start and end apart: 5 -> 0, of which waited for: 5 -> 0; matrix products, arithmetic and copies ran while one was open for 19% -> 0% of each run, Pallas kernels for 0% -> 0%
where the time goes in v1:
time: 87.7 us; the launch traced here: 87.5 us
  Pallas kernels  79.5 us (91%)
  local copies, waits for them, and re-layouts  7.42 us (8%)
    pallas_call x1, Pallas kernels, per_device(): pl.pallas_call(kernel, out_shape=(jax.ShapeDtypeStruct((TOK, 1024), BF16)...  79.5 us
    unnamed x13, local copies, waits for them, and re-layouts  7.42 us

profile of v1, /device:TPU:1, one launch (start us, length us, event | category | flops | bytes accessed | tf_op | source)
XLA Modules:
  0.0 87.5 jit_solution(13841689421813341988)
XLA Ops:
  0.6 79.5 %shard_map.92 = (bf16[1024,1024]{1,0:T(8,128)(2,1)}, bf16[1024,512]{1,0:T(8,128)(2,1)}, bf16[1024,512]{1,0:T(8,128)(2,1)}, bf16[1024,512]{1,0:T(8,128)(2,1)}, f32[128,512]{1,0:T(8,128)}) custom-call(bf16[1024,512]{1,0:T(8,128)(2,1)} %q_hbm.1, bf16[1024,512]{1,0:T(8,128)(2,1)} %k_hbm.1, bf16[1024,512]{1,0:T(8,128)(2,1)} %v_hbm.1, bf16[128,512]{1,0:T(8,128)(2,1)} %w_hbm.1, ...), custom_call_target="tpu_custom_call" | custom-call | tf_op jit(solution)/shard_map/pallas_call | solution.py:573
  80.1 0.0 copy-start.2
  80.1 3.2 %copy.15 = bf16[1024,1024]{1,0:T(8,128)(2,1)} copy(bf16[1024,1024]{1,0:T(8,128)(2,1)} %get-tuple-element.10) | data formatting | bytes 4194304
  83.3 0.0 copy-done.2
  83.3 0.0 copy-start.1
  83.3 0.0 copy-start
  83.3 1.0 %copy.16 = bf16[1024,512]{1,0:T(8,128)(2,1)} copy(bf16[1024,512]{1,0:T(8,128)(2,1)S(1)} %copy-done.2) | data formatting | bytes 2097152
  84.3 0.6 copy-done.1
  84.9 0.0 copy-start.3
  84.9 1.0 %copy.17 = bf16[1024,512]{1,0:T(8,128)(2,1)} copy(bf16[1024,512]{1,0:T(8,128)(2,1)S(1)} %copy-done.1) | data formatting | bytes 2097152
  85.9 0.0 copy-done
  85.9 1.0 %copy.18 = bf16[1024,512]{1,0:T(8,128)(2,1)} copy(bf16[1024,512]{1,0:T(8,128)(2,1)S(1)} %copy-done) | data formatting | bytes 2097152
  86.8 0.0 copy-done.3
  86.8 0.7 copy.19
Async XLA Ops:
  80.1 3.2 %copy-start.2 = (bf16[1024,512]{1,0:T(8,128)(2,1)S(1)}, bf16[1024,512]{1,0:T(8,128)(2,1)}, u32[]{:S(2)}) copy-start(bf16[1024,512]{1,0:T(8,128)(2,1)} %get-tuple-element.11) | copy-start | bytes 3145732
  83.3 1.6 %copy-start.1 = (bf16[1024,512]{1,0:T(8,128)(2,1)S(1)}, bf16[1024,512]{1,0:T(8,128)(2,1)}, u32[]{:S(2)}) copy-start(bf16[1024,512]{1,0:T(8,128)(2,1)} %get-tuple-element.12) | copy-start | bytes 3145732
  83.3 2.6 %copy-start = (bf16[1024,512]{1,0:T(8,128)(2,1)S(1)}, bf16[1024,512]{1,0:T(8,128)(2,1)}, u32[]{:S(2)}) copy-start(bf16[1024,512]{1,0:T(8,128)(2,1)} %get-tuple-element.13) | copy-start | bytes 3145732
  84.9 1.9 %copy-start.3 = (f32[128,512]{1,0:T(8,128)S(1)}, f32[128,512]{1,0:T(8,128)}, u32[]{:S(2)}) copy-start(f32[128,512]{1,0:T(8,128)} %get-tuple-element.14) | copy-start | bytes 786436

commit v2 on v1

v2 whole, which is shorter than its diff:
```python
import jax
import jax.numpy as jnp
from jax import lax
from jax.experimental import pallas as pl
from jax.experimental.pallas import tpu as pltpu
from jax.sharding import PartitionSpec as P

HEAD_DIM = 128
HEADS = 4
CHUNK = 256
CHUNKS = 4
TOK = 1024
COLS = 512
WIDTH = 4096
EPSILON = 1e-06
MESH = pl.DeviceIdType.MESH
F32 = jnp.float32
BF16 = jnp.bfloat16


def nn(a, b):
    return lax.dot_general(a, b, (((1,), (0,)), ((), ())), preferred_element_type=F32)


def nt(a, b):
    return lax.dot_general(a, b, (((1,), (1,)), ((), ())), preferred_element_type=F32)


def tn(a, b):
    return lax.dot_general(a, b, (((0,), (0,)), ((), ())), preferred_element_type=F32)


def kernel(
    q_hbm, k_hbm, v_hbm, w_hbm, og_hbm,
    mixed_hbm, gq_hbm, gk_hbm, gv_hbm, gw_hbm,
    q, k, v, og, wc, quarter, wr, nb, normed_t, masked_t, att, nf, inv,
    kvs, states, ga, qdas, futures, own_state, peer, chip_state, slices, offset, before, back, final,
    pt, r0, ra, rb, qa, qb, r2a, r2b, acc, mixed, gq, gk, gv, gw,
    load_sem, out_sem,
    wc1_s, wc1_r, wc2_s, wc2_r, wcs_s, wcs_r,
    wq_s, wq_r, wz_s, wz_r, wr1_s, wr1_r, wr2_s, wr2_r, wrs_s, wrs_r,
    sc1_s, sc1_r, sc2_s, sc2_r, sc3_s, sc3_r, sc4_s, sc4_r,
    zs_s, zs_r, zf_s, zf_r,
    rs0_s, rs0_r, rs1_s, rs1_r, rs2_s, rs2_r,
):
    seq = lax.axis_index("seq")
    z = lax.axis_index("head")
    x, y, c = seq // 8, (seq // 2) % 4, seq % 2
    chip = x * 4 + y

    def at(x_, y_, c_, z_):
        return (x_ * 8 + y_ * 2 + c_, z_)

    def x_dev(d):
        return at((x + d) % 4, y, c, z)

    def y_dev(d):
        return at(x, (y + d) % 4, c, z)

    def z_dev(d):
        return (seq, (z + d) % 4)

    def plane_dev(m):
        other = (chip + m) % 16
        return at(other // 4, other % 4, c, z)

    sibling = at(x, y, 1 - c, z)

    def remote(src, dst, send, recv, device):
        return pltpu.make_async_remote_copy(
            src_ref=src, dst_ref=dst, send_sem=send, recv_sem=recv,
            device_id=device, device_id_type=MESH,
        )

    pending = []

    def go(copies):
        for copy in copies:
            copy.start()
            pending.append(copy)
        return copies

    def arrived(copies):
        for copy in copies:
            copy.wait_recv()

    loads = [
        pltpu.make_async_copy(w_hbm, wc.at[x, y, c], load_sem.at[0]),
        pltpu.make_async_copy(k_hbm, k, load_sem.at[1]),
        pltpu.make_async_copy(v_hbm, v, load_sem.at[2]),
        pltpu.make_async_copy(q_hbm, q, load_sem.at[3]),
        pltpu.make_async_copy(og_hbm, og, load_sem.at[4]),
    ]
    for load in loads[:4]:
        load.start()

    barrier = pltpu.get_barrier_semaphore()
    partners = [plane_dev(m) for m in range(1, 16)] + [sibling, z_dev(1), z_dev(2), z_dev(3)]
    for partner in partners:
        pl.semaphore_signal(barrier, inc=1, device_id=partner, device_id_type=MESH)

    def rows_of(t):
        return pl.ds(pl.multiple_of(t * CHUNK, CHUNK), CHUNK)

    def head_cols(h):
        return slice(h * HEAD_DIM, (h + 1) * HEAD_DIM)

    loads[1].wait()
    loads[2].wait()
    loads[3].wait()
    loads[4].start()

    @pl.loop(0, CHUNKS)
    def _(t):
        for h in range(HEADS):
            kvs[t, h] = tn(k[rows_of(t), head_cols(h)], v[rows_of(t), head_cols(h)])

    def publish(n, source):
        for h in range(HEADS):
            state = source[0, h] + source[1, h] + source[2, h] + source[3, h]
            own_state[n, h // 2, (h % 2) * 8:(h % 2) * 8 + 8] = (
                state.astype(BF16).reshape(8, 16, HEAD_DIM)
            )

    def scan_first(n):
        return go(
            [remote(own_state.at[n, 1 - c], peer.at[n], sc1_s.at[n, 0], sc1_r.at[n, 0], sibling)]
        )

    def scan_second(n):
        chip_state[n] = (own_state[n, c].astype(F32) + peer[n].astype(F32)).astype(BF16)
        for m in range(1, 16):
            remote(
                chip_state.at[n, (chip + m) % 16], slices.at[n, chip],
                sc2_s.at[n], sc2_r.at[n], plane_dev(m),
            ).start()
        whole = remote(
            chip_state.at[n, pl.ds(0, 15)], slices.at[n, pl.ds(0, 15)],
            sc2_s.at[n], sc2_r.at[n], plane_dev(1),
        )
        pending.append(whole)
        slices[n, chip] = chip_state[n, chip]
        return [whole]

    def scan_third(n):
        base = jnp.zeros((16, HEAD_DIM), F32)
        for i in range(16) if n == 0 else range(15, -1, -1):
            offset[n, i] = base.astype(BF16)
            base = base + slices[n, i].astype(F32)
        for m in range(1, 16):
            remote(
                offset.at[n, (chip + m) % 16], before.at[n, chip],
                sc3_s.at[n], sc3_r.at[n], plane_dev(m),
            ).start()
        whole = remote(
            offset.at[n, pl.ds(0, 15)], before.at[n, pl.ds(0, 15)],
            sc3_s.at[n], sc3_r.at[n], plane_dev(1),
        )
        pending.append(whole)
        before[n, chip] = offset[n, chip]
        return [whole]

    def scan_fourth(n):
        base = before[n].astype(F32)
        self_second, other_second = (c == 1, c == 0) if n == 0 else (c == 0, c == 1)
        back[n] = (base + jnp.where(other_second, own_state[n, c].astype(F32), 0.0)).astype(BF16)
        copies = go(
            [remote(back.at[n], final.at[n, c], sc4_s.at[n, 0], sc4_r.at[n, 0], sibling)]
        )
        final[n, c] = (base + jnp.where(self_second, peer[n].astype(F32), 0.0)).astype(BF16)
        return copies

    def incoming(n, h):
        half = final[n, h // 2, (h % 2) * 8:(h % 2) * 8 + 8].astype(F32)
        return half.reshape(HEAD_DIM, HEAD_DIM)

    publish(0, kvs)
    pl.semaphore_wait(barrier, len(partners))
    step = scan_first(0)

    loads[0].wait()
    wc_first = go(
        [
            remote(
                wc.at[x, y, c, pl.ds(0, 64)], wc.at[x, y, c, pl.ds(0, 64)],
                wc1_s.at[d - 1], wc1_r.at[d - 1], x_dev(d),
            )
            for d in (1, 3, 2)
        ]
        + [
            remote(
                wc.at[x, y, c, pl.ds(64, 64)], wc.at[x, y, c, pl.ds(64, 64)],
                wc1_s.at[2 + d], wc1_r.at[2 + d], y_dev(d),
            )
            for d in (1, 3, 2)
        ]
    )

    def quarter_rows(part):
        return pl.ds(pl.multiple_of(part * 32, 32), 32)

    quarters = go(
        [
            remote(
                wc.at[x, y, c, quarter_rows((x + d) % 4)], quarter.at[x],
                wq_s.at[d - 1], wq_r.at[d - 1], x_dev(d),
            )
            for d in (1, 3, 2)
        ]
    )
    quarter[x] = wc[x, y, c, quarter_rows(x), :]

    row = lax.broadcasted_iota(jnp.int32, (CHUNK, CHUNK), 0)
    col = lax.broadcasted_iota(jnp.int32, (CHUNK, CHUNK), 1)

    def lower(scores):
        return jnp.where(row >= col, scores, 0.0).astype(BF16)

    def upper(scores):
        return jnp.where(row <= col, scores, 0.0).astype(BF16)

    def intra(t):
        for h in range(HEADS):
            qh, kh = q[rows_of(t), head_cols(h)], k[rows_of(t), head_cols(h)]
            att[rows_of(t), head_cols(h)] = nn(lower(nt(qh, kh)), v[rows_of(t), head_cols(h)])

    pl.loop(0, 1)(intra)
    arrived(step)
    step = scan_second(0)
    pl.loop(1, CHUNKS)(intra)
    arrived(step)
    step = scan_third(0)
    arrived(wc_first)
    arrived(quarters)

    wc_second = go(
        [
            remote(
                wc.at[:, y, c, pl.ds(0, 64)], wc.at[:, y, c, pl.ds(0, 64)],
                wc2_s.at[d - 1], wc2_r.at[d - 1], y_dev(d),
            )
            for d in (1, 3, 2)
        ]
        + [
            remote(
                wc.at[x, :, c, pl.ds(64, 64)], wc.at[x, :, c, pl.ds(64, 64)],
                wc2_s.at[2 + d], wc2_r.at[2 + d], x_dev(d),
            )
            for d in (1, 3, 2)
        ]
    )

    to_layer = go(
        [
            remote(
                quarter.at[(z + d) % 4], wr.at[3 - d, y, c, x],
                wz_s.at[d - 1], wz_r.at[d - 1], z_dev(d),
            )
            for d in (1, 3, 2)
        ]
    )

    @pl.loop(0, CHUNKS)
    def _(t):
        for h in range(HEADS):
            masked_t[t, h] = upper(nt(k[rows_of(t), head_cols(h)], q[rows_of(t), head_cols(h)]))

    arrived(step)
    step = scan_fourth(0)
    arrived(step)

    for h in range(HEADS):
        state = incoming(0, h)
        for t in range(CHUNKS):
            states[t, h] = state.astype(BF16)
            state = state + kvs[t, h]

    def z_send(t, way):
        return remote(
            nb.at[0, rows_of(t)], nb.at[3 if way == 0 else 1, rows_of(t)],
            zs_s.at[way, t], zs_r.at[way, t], z_dev(1 if way == 0 else 3),
        )

    def z_forward(t, way):
        part = pl.ds(pl.multiple_of(t * CHUNK + way * 128, 128), 128)
        return remote(
            nb.at[3 if way == 0 else 1, part], nb.at[2, part],
            zf_s.at[way, t], zf_r.at[way, t], z_dev(1 if way == 0 else 3),
        )

    def forward(t):
        for way in (0, 1):
            z_send(t, way).wait_recv()
            z_forward(t, way).start()

    @pl.loop(0, CHUNKS)
    def _(t):
        for h in range(HEADS):
            a = att[rows_of(t), head_cols(h)] + nn(q[rows_of(t), head_cols(h)], states[t, h])
            scale = lax.rsqrt(jnp.mean(a * a, axis=-1, keepdims=True) + EPSILON)
            n = a * scale
            nf[rows_of(t), head_cols(h)] = n
            inv[rows_of(t), head_cols(h)] = jnp.broadcast_to(scale, n.shape)
            nb[0, rows_of(t), head_cols(h)] = n.astype(BF16)
            normed_t[head_cols(h), rows_of(t)] = n.T.astype(BF16)
        for way in (0, 1):
            z_send(t, way).start()

    arrived(to_layer)
    wr_first = go(
        [
            remote(
                wr.at[:, y, c, x, pl.ds(0, 16)], wr.at[:, y, c, x, pl.ds(0, 16)],
                wr1_s.at[d - 1], wr1_r.at[d - 1], x_dev(d),
            )
            for d in (1, 3, 2)
        ]
        + [
            remote(
                wr.at[:, y, c, x, pl.ds(16, 16)], wr.at[:, y, c, x, pl.ds(16, 16)],
                wr1_s.at[2 + d], wr1_r.at[2 + d], y_dev(d),
            )
            for d in (1, 3, 2)
        ]
    )

    def pair_copy(i):
        return remote(
            pt.at[i, :, 1 - c], r0.at[i], rs0_s.at[i], rs0_r.at[i], sibling
        )

    loads[4].wait()

    def term(i, two):
        block = og[:, pl.ds(pl.multiple_of((i * 2 + two) * 512, 512), 512)]
        result = nn(normed_t[...], block).astype(BF16)
        for n in range(4):
            pt[i, two * 2 + n // 2, n % 2] = result[:, n * 128:(n + 1) * 128]

    def terms(d):
        i = (x + d) % 4
        pl.loop(0, 2)(lambda two: term(i, two))
        pair_copy(i).start()

    terms(1)
    terms(2)
    arrived(wc_second)
    wc_last = go([remote(wc.at[:, :, c], wc.at[:, :, c], wcs_s.at[0], wcs_r.at[0], sibling)])

    arrived(wr_first)
    wr_second = go(
        [
            remote(
                wr.at[:, y, c, :, pl.ds(0, 16)], wr.at[:, y, c, :, pl.ds(0, 16)],
                wr2_s.at[d - 1], wr2_r.at[d - 1], y_dev(d),
            )
            for d in (1, 3, 2)
        ]
        + [
            remote(
                wr.at[:, :, c, x, pl.ds(16, 16)], wr.at[:, :, c, x, pl.ds(16, 16)],
                wr2_s.at[2 + d], wr2_r.at[2 + d], x_dev(d),
            )
            for d in (1, 3, 2)
        ]
    )

    terms(3)

    arrived(wc_last)

    @pl.loop(0, 2)
    def _(two):
        both = pl.ds(pl.multiple_of(two * 512, 512), 512)
        g_all = nn(og[both, :], wc[...].reshape(WIDTH, COLS))
        for part in range(2):
            t = two * 2 + part
            for h in range(HEADS):
                g = g_all[part * CHUNK:(part + 1) * CHUNK, head_cols(h)]
                n = nf[rows_of(t), head_cols(h)]
                inner = jnp.mean(n * g, axis=-1, keepdims=True)
                grad = (inv[rows_of(t), head_cols(h)] * (g - n * inner)).astype(BF16)
                ga[rows_of(t), head_cols(h)] = grad
                qdas[t, h] = tn(q[rows_of(t), head_cols(h)], grad)

    publish(1, qdas)
    step = scan_first(1)
    forward(0)
    forward(1)

    def inner_gradients(t):
        for h in range(HEADS):
            where = (rows_of(t), head_cols(h))
            qh, kh, vh, gh = q[where], k[where], v[where], ga[where]
            dmask = lower(nt(gh, vh))
            gq[where] = (nn(dmask, kh) + nt(gh, states[t, h])).astype(BF16)
            dmask_t = upper(nt(vh, gh))
            att[where] = nn(dmask_t, qh)
            nf[where] = nn(masked_t[t, h], gh)

    def x_final(d):
        return remote(
            qb.at[(x + d) % 4], r2b.at[d - 1], rs2_s.at[1, d - 1], rs2_r.at[1, d - 1], x_dev(d)
        )

    def y_final(d):
        return remote(
            qa.at[(y + d) % 4], r2a.at[d - 1], rs2_s.at[0, d - 1], rs2_r.at[0, d - 1], y_dev(d)
        )

    terms(0)
    arrived(step)
    step = scan_second(1)
    pl.loop(0, 3)(inner_gradients)
    arrived(step)
    step = scan_third(1)

    def x_part(d):
        return remote(
            pt.at[(x + d) % 4, :, c, pl.ds(0, 256)], ra.at[d - 1],
            rs1_s.at[0, d - 1], rs1_r.at[0, d - 1], x_dev(d),
        )

    for d in range(1, 5):
        i = (x + d) % 4
        pair_copy(i).wait_recv()

        @pl.loop(0, 4)
        def _(j):
            pt[i, j, c] = (pt[i, j, c].astype(F32) + r0[i, j].astype(F32)).astype(BF16)

        if d < 4:
            x_part(d).start()

    def y_part(d):
        return remote(
            pt.at[:, (y + d) % 4, c, pl.ds(256, 256)], rb.at[d - 1],
            rs1_s.at[1, d - 1], rs1_r.at[1, d - 1], y_dev(d),
        )

    for d in (1, 3, 2):
        y_part(d).start()

    pl.loop(3, CHUNKS)(inner_gradients)
    forward(2)
    forward(3)
    arrived(wr_second)
    wr_last = go([remote(wr.at[:, :, c], wr.at[:, :, c], wrs_s.at[0], wrs_r.at[0], sibling)])
    arrived(step)
    step = scan_fourth(1)
    arrived(step)

    for h in range(HEADS):
        state = incoming(1, h)
        for t in range(CHUNKS - 1, -1, -1):
            futures[t, h] = state.astype(BF16)
            state = state + qdas[t, h]

    @pl.loop(0, CHUNKS)
    def _(t):
        for h in range(HEADS):
            where = (rows_of(t), head_cols(h))
            gk[where] = (att[where] + nt(v[where], futures[t, h])).astype(BF16)
            gv[where] = (nf[where] + nn(k[where], futures[t, h])).astype(BF16)

    stores = [
        pltpu.make_async_copy(gq, gq_hbm, out_sem.at[0]),
        pltpu.make_async_copy(gk, gk_hbm, out_sem.at[1]),
        pltpu.make_async_copy(gv, gv_hbm, out_sem.at[2]),
    ]
    for store in stores:
        store.start()

    arrived(wr_last)

    @pl.loop(0, 2)
    def _(two):
        both = pl.ds(pl.multiple_of(two * 512, 512), 512)
        result = nt(nb[0, both], wc[z].reshape(TOK, COLS))
        for d in (1, 3):
            result = result + nt(nb[d, both], wr[d - 1].reshape(TOK, COLS))
        acc[both, :] = result

    for d in range(1, 4):
        x_part(d).wait_recv()
    for j in range(4):
        summed = pt[x, j, c, :256, :].astype(F32)
        for d in range(3):
            summed = summed + ra[d, j].astype(F32)
        qa[j] = summed.astype(BF16)

    finals = go([y_final(d) for d in (1, 3, 2)])
    for d in range(1, 4):
        y_part(d).wait_recv()
    for j in range(4):
        summed = pt[j, y, c, 256:, :].astype(F32)
        for d in range(3):
            summed = summed + rb[d, j].astype(F32)
        qb[j] = summed.astype(BF16)
    finals += go([x_final(d) for d in (1, 3, 2)])
    def out_copy(t):
        return pltpu.make_async_copy(
            mixed.at[rows_of(t)], mixed_hbm.at[rows_of(t)], out_sem.at[4 + t]
        )

    @pl.loop(0, CHUNKS)
    def _(t):
        for way in (0, 1):
            z_forward(t, way).wait_recv()
        result = acc[rows_of(t), :] + nt(nb[2, rows_of(t)], wr[1].reshape(TOK, COLS))
        mixed[rows_of(t), :] = result.astype(BF16)
        out_copy(t).start()

    arrived(finals)
    for half, own, others in ((0, qa[y], r2a), (1, qb[x], r2b)):
        summed = own.astype(F32)
        for d in range(3):
            summed = summed + others[d].astype(F32)
        gw[:, half * 256:(half + 1) * 256] = summed.T
    stores.append(pltpu.make_async_copy(gw, gw_hbm, out_sem.at[3]))
    stores[-1].start()

    for copy in pending:
        copy.wait_send()

    @pl.loop(0, CHUNKS)
    def _(t):
        for way in (0, 1):
            z_send(t, way).wait_send()
            z_forward(t, way).wait_send()
        out_copy(t).wait()

    for i in range(4):
        pair_copy(i).wait_send()

    for d in range(1, 4):
        x_part(d).wait_send()
        y_part(d).wait_send()
    for store in stores:
        store.wait()


def deliver(*refs):
    sources, targets, held = refs[:5], refs[5:10], refs[10:15]
    in_sem, out_sem = refs[15:]
    pieces = []
    for a, source in enumerate(sources):
        rows = source.shape[0] // 4
        for part in range(4):
            at = pl.ds(part * rows, rows)
            n = a * 4 + part
            pieces.append(
                (
                    pltpu.make_async_copy(source.at[at], held[a].at[at], in_sem.at[n]),
                    pltpu.make_async_copy(held[a].at[at], targets[a].at[at], out_sem.at[n]),
                )
            )
    for load, _ in pieces:
        load.start()
    for load, store in pieces:
        load.wait()
        store.start()
    for _, store in pieces:
        store.wait()


def per_device(queries, keys, values, out_weight, out_grad):
    dma = pltpu.SemaphoreType.DMA
    vm = pltpu.VMEM
    scratch = [
        vm((TOK, COLS), BF16),
        vm((TOK, COLS), BF16),
        vm((TOK, COLS), BF16),
        vm((TOK, WIDTH), BF16),
        vm((4, 4, 2, 128, COLS), BF16),
        vm((4, 32, COLS), BF16),
        vm((3, 4, 2, 4, 32, COLS), BF16),
        vm((4, TOK, COLS), BF16),
        vm((COLS, TOK), BF16),
        vm((CHUNKS, HEADS, CHUNK, CHUNK), BF16),
        vm((TOK, COLS), F32),
        vm((TOK, COLS), F32),
        vm((TOK, COLS), F32),
        vm((CHUNKS, HEADS, 128, 128), F32),
        vm((CHUNKS, HEADS, 128, 128), BF16),
        vm((TOK, COLS), BF16),
        vm((CHUNKS, HEADS, 128, 128), F32),
        vm((CHUNKS, HEADS, 128, 128), BF16),
        vm((2, 2, 16, 16, 128), BF16),
        vm((2, 16, 16, 128), BF16),
        vm((2, 16, 16, 128), BF16),
        vm((2, 16, 16, 128), BF16),
        vm((2, 16, 16, 128), BF16),
        vm((2, 16, 16, 128), BF16),
        vm((2, 16, 16, 128), BF16),
        vm((2, 2, 16, 16, 128), BF16),
        vm((4, 4, 2, COLS, 128), BF16),
        vm((4, 4, COLS, 128), BF16),
        vm((3, 4, 256, 128), BF16),
        vm((3, 4, 256, 128), BF16),
        vm((4, 256, 128), BF16),
        vm((4, 256, 128), BF16),
        vm((3, 256, 128), BF16),
        vm((3, 256, 128), BF16),
        vm((TOK, 1024), F32),
        vm((TOK, 1024), BF16),
        vm((TOK, COLS), BF16),
        vm((TOK, COLS), BF16),
        vm((TOK, COLS), BF16),
        vm((128, COLS), F32),
        dma((5,)),
        dma((8,)),
    ]
    pairs = [
        (6,), (6,), (1,),
        (3,), (3,), (6,), (6,), (1,),
        (2, 1), (2,), (2,), (2, 1),
        (2, CHUNKS), (2, CHUNKS),
        (4,), (2, 3), (2, 3),
    ]
    for shape in pairs:
        scratch += [dma(shape), dma(shape)]
    anywhere = pl.BlockSpec(memory_space=pl.ANY)
    shapes = (
        jax.ShapeDtypeStruct((TOK, 1024), BF16),
        jax.ShapeDtypeStruct((TOK, COLS), BF16),
        jax.ShapeDtypeStruct((TOK, COLS), BF16),
        jax.ShapeDtypeStruct((TOK, COLS), BF16),
        jax.ShapeDtypeStruct((128, COLS), F32),
    )
    results = pl.pallas_call(
        kernel,
        out_shape=shapes,
        in_specs=[anywhere] * 5,
        out_specs=(anywhere,) * 5,
        scratch_shapes=scratch,
        compiler_params=pltpu.CompilerParams(
            collective_id=0, has_side_effects=True, vmem_limit_bytes=60 << 20
        ),
    )(queries, keys, values, out_weight, out_grad)
    return pl.pallas_call(
        deliver,
        out_shape=shapes,
        in_specs=[anywhere] * 5,
        out_specs=(anywhere,) * 5,
        scratch_shapes=[vm(shape.shape, shape.dtype) for shape in shapes] + [dma((20,)), dma((20,))],
        compiler_params=pltpu.CompilerParams(vmem_limit_bytes=60 << 20),
    )(*results)


def solution(mesh):
    in_specs = (
        P("seq", "head"),
        P("seq", "head"),
        P("seq", "head"),
        P("seq", "head"),
        P("seq", None),
    )
    out_specs = (
        P("seq", "head"),
        P("seq", "head"),
        P("seq", "head"),
        P("seq", "head"),
        P("seq", "head"),
    )
    return jax.shard_map(
        per_device, mesh=mesh, in_specs=in_specs, out_specs=out_specs, check_vma=False
    )
```

time: 87.7 us -> 75 us (0.86)
  local copies, waits for them, and re-layouts: 7.42 us -> 0 us
  Pallas kernels: 79.5 us -> 74.2 us
    unnamed x13 -> x0, local copies, waits for them, and re-layouts: 7.42 us -> none
    pallas_call x1 -> x2, Pallas kernels: 79.5 us -> 74.2 us  [the longest x1 69.3 us: per_device(): pl.pallas_call(kernel, out_shape=shapes, in_specs=[anywhere] * 5, out_spe...]
where the time goes in v2:
time: 75 us; the launch traced here: 74.9 us
  Pallas kernels  74.2 us (99%)
    pallas_call x1, Pallas kernels, per_device(): pl.pallas_call(kernel, out_shape=shapes, in_specs=[anywhere] * 5, out_spe...  69.3 us
    pallas_call x1, Pallas kernels, per_device(): pl.pallas_call(deliver, out_shape=shapes, in_specs=[anywhere] * 5, out_sp...  4.92 us

profile of v2, /device:TPU:1, one launch (start us, length us, event | category | flops | bytes accessed | tf_op | source)
XLA Modules:
  0.0 74.9 jit_solution(11123504084794681436)
XLA Ops:
  0.6 69.3 %shard_map.92 = (bf16[1024,1024]{1,0:T(8,128)(2,1)}, bf16[1024,512]{1,0:T(8,128)(2,1)}, bf16[1024,512]{1,0:T(8,128)(2,1)}, bf16[1024,512]{1,0:T(8,128)(2,1)}, f32[128,512]{1,0:T(8,128)}) custom-call(bf16[1024,512]{1,0:T(8,128)(2,1)} %q_hbm.1, bf16[1024,512]{1,0:T(8,128)(2,1)} %k_hbm.1, bf16[1024,512]{1,0:T(8,128)(2,1)} %v_hbm.1, bf16[128,512]{1,0:T(8,128)(2,1)} %w_hbm.1, ...), custom_call_target="tpu_custom_call" | custom-call | tf_op jit(solution)/shard_map/pallas_call | solution.py:631
  70.0 4.9 %shard_map.93 = (bf16[1024,1024]{1,0:T(8,128)(2,1)}, bf16[1024,512]{1,0:T(8,128)(2,1)}, bf16[1024,512]{1,0:T(8,128)(2,1)}, bf16[1024,512]{1,0:T(8,128)(2,1)}, f32[128,512]{1,0:T(8,128)}) custom-call(bf16[1024,1024]{1,0:T(8,128)(2,1)} %get-tuple-element.10.refs_0_, bf16[1024,512]{1,0:T(8,128)(2,1)} %get-tuple-element.11.refs_1_, ...), custom_call_target="tpu_custom_call" | custom-call | tf_op jit(solution)/shard_map/pallas_call | solution.py:641

commit v3 on v2

--- a/solution.py
+++ b/solution.py
@@ -32,11 +32,11 @@
 
 def kernel(
     q_hbm, k_hbm, v_hbm, w_hbm, og_hbm,
-    mixed_hbm, gq_hbm, gk_hbm, gv_hbm, gw_hbm,
+    mixed, gq, gk, gv, gw,
     q, k, v, og, wc, quarter, wr, nb, normed_t, masked_t, att, nf, inv,
     kvs, states, ga, qdas, futures, own_state, peer, chip_state, slices, offset, before, back, final,
-    pt, r0, ra, rb, qa, qb, r2a, r2b, acc, mixed, gq, gk, gv, gw,
-    load_sem, out_sem,
+    pt, r0, ra, rb, qa, qb, r2a, r2b, acc,
+    load_sem,
     wc1_s, wc1_r, wc2_s, wc2_r, wcs_s, wcs_r,
     wq_s, wq_r, wz_s, wz_r, wr1_s, wr1_r, wr2_s, wr2_r, wrs_s, wrs_r,
     sc1_s, sc1_r, sc2_s, sc2_r, sc3_s, sc3_r, sc4_s, sc4_r,
@@ -339,7 +339,8 @@
 
     def terms(d):
         i = (x + d) % 4
-        pl.loop(0, 2)(lambda two: term(i, two))
+        for two in range(2):
+            term(i, two)
         pair_copy(i).start()
 
     terms(1)
@@ -463,14 +464,6 @@
             gk[where] = (att[where] + nt(v[where], futures[t, h])).astype(BF16)
             gv[where] = (nf[where] + nn(k[where], futures[t, h])).astype(BF16)
 
-    stores = [
-        pltpu.make_async_copy(gq, gq_hbm, out_sem.at[0]),
-        pltpu.make_async_copy(gk, gk_hbm, out_sem.at[1]),
-        pltpu.make_async_copy(gv, gv_hbm, out_sem.at[2]),
-    ]
-    for store in stores:
-        store.start()
-
     arrived(wr_last)
 
     @pl.loop(0, 2)
@@ -498,18 +491,12 @@
             summed = summed + rb[d, j].astype(F32)
         qb[j] = summed.astype(BF16)
     finals += go([x_final(d) for d in (1, 3, 2)])
-    def out_copy(t):
-        return pltpu.make_async_copy(
-            mixed.at[rows_of(t)], mixed_hbm.at[rows_of(t)], out_sem.at[4 + t]
-        )
-
     @pl.loop(0, CHUNKS)
     def _(t):
         for way in (0, 1):
             z_forward(t, way).wait_recv()
         result = acc[rows_of(t), :] + nt(nb[2, rows_of(t)], wr[1].reshape(TOK, COLS))
         mixed[rows_of(t), :] = result.astype(BF16)
-        out_copy(t).start()
 
     arrived(finals)
     for half, own, others in ((0, qa[y], r2a), (1, qb[x], r2b)):
@@ -517,8 +504,6 @@
         for d in range(3):
             summed = summed + others[d].astype(F32)
         gw[:, half * 256:(half + 1) * 256] = summed.T
-    stores.append(pltpu.make_async_copy(gw, gw_hbm, out_sem.at[3]))
-    stores[-1].start()
 
     for copy in pending:
         copy.wait_send()
@@ -528,7 +513,6 @@
         for way in (0, 1):
             z_send(t, way).wait_send()
             z_forward(t, way).wait_send()
-        out_copy(t).wait()
 
     for i in range(4):
         pair_copy(i).wait_send()
@@ -536,32 +520,17 @@
     for d in range(1, 4):
         x_part(d).wait_send()
         y_part(d).wait_send()
-    for store in stores:
-        store.wait()
 
 
 def deliver(*refs):
-    sources, targets, held = refs[:5], refs[5:10], refs[10:15]
-    in_sem, out_sem = refs[15:]
-    pieces = []
-    for a, source in enumerate(sources):
-        rows = source.shape[0] // 4
-        for part in range(4):
-            at = pl.ds(part * rows, rows)
-            n = a * 4 + part
-            pieces.append(
-                (
-                    pltpu.make_async_copy(source.at[at], held[a].at[at], in_sem.at[n]),
-                    pltpu.make_async_copy(held[a].at[at], targets[a].at[at], out_sem.at[n]),
-                )
-            )
-    for load, _ in pieces:
-        load.start()
-    for load, store in pieces:
-        load.wait()
-        store.start()
-    for _, store in pieces:
-        store.wait()
+    copies = [
+        pltpu.make_async_copy(source, target, refs[10].at[i])
+        for i, (source, target) in enumerate(zip(refs[:5], refs[5:10]))
+    ]
+    for copy in copies:
+        copy.start()
+    for copy in copies:
+        copy.wait()
 
 
 def per_device(queries, keys, values, out_weight, out_grad):
@@ -603,13 +572,7 @@
         vm((3, 256, 128), BF16),
         vm((3, 256, 128), BF16),
         vm((TOK, 1024), F32),
-        vm((TOK, 1024), BF16),
-        vm((TOK, COLS), BF16),
-        vm((TOK, COLS), BF16),
-        vm((TOK, COLS), BF16),
-        vm((128, COLS), F32),
         dma((5,)),
-        dma((8,)),
     ]
     pairs = [
         (6,), (6,), (1,),
@@ -630,21 +593,21 @@
     )
     results = pl.pallas_call(
         kernel,
-        out_shape=shapes,
+        out_shape=tuple(vm(shape.shape, shape.dtype) for shape in shapes),
         in_specs=[anywhere] * 5,
-        out_specs=(anywhere,) * 5,
+        out_specs=(pl.BlockSpec(memory_space=vm),) * 5,
         scratch_shapes=scratch,
         compiler_params=pltpu.CompilerParams(
-            collective_id=0, has_side_effects=True, vmem_limit_bytes=60 << 20
+            collective_id=0, has_side_effects=True, vmem_limit_bytes=52 << 20
         ),
     )(queries, keys, values, out_weight, out_grad)
     return pl.pallas_call(
         deliver,
         out_shape=shapes,
-        in_specs=[anywhere] * 5,
+        in_specs=[pl.BlockSpec(memory_space=vm)] * 5,
         out_specs=(anywhere,) * 5,
-        scratch_shapes=[vm(shape.shape, shape.dtype) for shape in shapes] + [dma((20,)), dma((20,))],
-        compiler_params=pltpu.CompilerParams(vmem_limit_bytes=60 << 20),
+        scratch_shapes=[dma((5,))],
+        compiler_params=pltpu.CompilerParams(vmem_limit_bytes=4 << 20),
     )(*results)
 
 

time: 75 us -> 70 us (0.933)
  Pallas kernels: 74.2 us -> 69.1 us
    pallas_call x2, Pallas kernels: 74.2 us -> 69.1 us  [the longest x1 66.7 us: per_device(): pl.pallas_call(kernel, out_shape=tuple((vm(shape.shape, shape.dtype) for...]
where the time goes in v3:
time: 70 us; the launch traced here: 69.8 us
  Pallas kernels  69.1 us (99%)
    pallas_call x1, Pallas kernels, per_device(): pl.pallas_call(kernel, out_shape=tuple((vm(shape.shape, shape.dtype) for...  66.7 us
    pallas_call x1, Pallas kernels, per_device(): pl.pallas_call(deliver, out_shape=shapes, in_specs=[pl.BlockSpec(memory_s...  2.45 us

profile of v3, /device:TPU:1, one launch (start us, length us, event | category | flops | bytes accessed | tf_op | source)
XLA Modules:
  0.0 69.8 jit_solution(713544030584417042)
XLA Ops:
  0.6 66.7 %shard_map.92 = (bf16[1024,1024]{1,0:T(8,128)(2,1)S(1)}, bf16[1024,512]{1,0:T(8,128)(2,1)S(1)}, bf16[1024,512]{1,0:T(8,128)(2,1)S(1)}, bf16[1024,512]{1,0:T(8,128)(2,1)S(1)}, f32[128,512]{1,0:T(8,128)S(1)}) custom-call(bf16[1024,512]{1,0:T(8,128)(2,1)} %q_hbm.1, bf16[1024,512]{1,0:T(8,128)(2,1)} %k_hbm.1, bf16[1024,512]{1,0:T(8,128)(2,1)} %v_hbm.1, ...), custom_call_target="tpu_custom_call" | custom-call | tf_op jit(solution)/shard_map/pallas_call | solution.py:594
  67.3 2.4 %shard_map.93 = (bf16[1024,1024]{1,0:T(8,128)(2,1)}, bf16[1024,512]{1,0:T(8,128)(2,1)}, bf16[1024,512]{1,0:T(8,128)(2,1)}, bf16[1024,512]{1,0:T(8,128)(2,1)}, f32[128,512]{1,0:T(8,128)}) custom-call(bf16[1024,1024]{1,0:T(8,128)(2,1)S(1)} %get-tuple-element.10.refs_0_, bf16[1024,512]{1,0:T(8,128)(2,1)S(1)} %get-tuple-element.11.refs_1_, ...), custom_call_target="tpu_custom_call" | custom-call | tf_op jit(solution)/shard_map/pallas_call | solution.py:604

commit v4 on v3

--- a/solution.py
+++ b/solution.py
@@ -345,6 +345,7 @@
 
     terms(1)
     terms(2)
+    terms(3)
     arrived(wc_second)
     wc_last = go([remote(wc.at[:, :, c], wc.at[:, :, c], wcs_s.at[0], wcs_r.at[0], sibling)])
 
@@ -366,7 +367,7 @@
         ]
     )
 
-    terms(3)
+    terms(0)
 
     arrived(wc_last)
 
@@ -409,7 +410,6 @@
             qa.at[(y + d) % 4], r2a.at[d - 1], rs2_s.at[0, d - 1], rs2_r.at[0, d - 1], y_dev(d)
         )
 
-    terms(0)
     arrived(step)
     step = scan_second(1)
     pl.loop(0, 3)(inner_gradients)

time: 70 us -> 68 us (0.971); the launches traced: 69.8 us -> 67.1 us
  Pallas kernels: 69.1 us -> 66.4 us
    pallas_call x1, Pallas kernels: 66.7 us -> 64 us  [per_device(): pl.pallas_call(kernel, out_shape=tuple((vm(shape.shape, shape.dtype) for...]
where the time goes in v4:
time: 68 us; the launch traced here: 67.1 us
  Pallas kernels  66.4 us (98%)
    pallas_call x1, Pallas kernels, per_device(): pl.pallas_call(kernel, out_shape=tuple((vm(shape.shape, shape.dtype) for...  64 us
    pallas_call x1, Pallas kernels, per_device(): pl.pallas_call(deliver, out_shape=shapes, in_specs=[pl.BlockSpec(memory_s...  2.45 us

profile of v4, /device:TPU:1, one launch (start us, length us, event | category | flops | bytes accessed | tf_op | source)
XLA Modules:
  0.0 67.1 jit_solution(5129386283188708984)
XLA Ops:
  0.6 64.0 %shard_map.92 = (bf16[1024,1024]{1,0:T(8,128)(2,1)S(1)}, bf16[1024,512]{1,0:T(8,128)(2,1)S(1)}, bf16[1024,512]{1,0:T(8,128)(2,1)S(1)}, bf16[1024,512]{1,0:T(8,128)(2,1)S(1)}, f32[128,512]{1,0:T(8,128)S(1)}) custom-call(bf16[1024,512]{1,0:T(8,128)(2,1)} %q_hbm.1, bf16[1024,512]{1,0:T(8,128)(2,1)} %k_hbm.1, bf16[1024,512]{1,0:T(8,128)(2,1)} %v_hbm.1, ...), custom_call_target="tpu_custom_call" | custom-call | tf_op jit(solution)/shard_map/pallas_call | solution.py:594
  64.6 2.4 %shard_map.93 = (bf16[1024,1024]{1,0:T(8,128)(2,1)}, bf16[1024,512]{1,0:T(8,128)(2,1)}, bf16[1024,512]{1,0:T(8,128)(2,1)}, bf16[1024,512]{1,0:T(8,128)(2,1)}, f32[128,512]{1,0:T(8,128)}) custom-call(bf16[1024,1024]{1,0:T(8,128)(2,1)S(1)} %get-tuple-element.10.refs_0_, bf16[1024,512]{1,0:T(8,128)(2,1)S(1)} %get-tuple-element.11.refs_1_, ...), custom_call_target="tpu_custom_call" | custom-call | tf_op jit(solution)/shard_map/pallas_call | solution.py:604
